TPU v7x, 128 devices: a whole 4x4x4 slice. The times are simulated.
128 devices in a mesh: row: 16 (over x, y), col: 8 (over z, core).
Axes of the slice: x: 4, y: 4, z: 4, core: 2. Of those that a mesh axis runs over, the one named last changes fastest.
Arguments:
- source_points: bfloat16 [65536, 1024], P('row'), may hold values from -8 to 8
- target_points: bfloat16 [32768, 1024], P('col', 'row'), may hold values from -8 to 8
- source_mass: float32 [65536], P('row'), may hold values from 0.25 to 4
- target_mass: float32 [32768], P('col'), may hold values from 0.25 to 4
- tile_index: int32 [256, 16], P('row', 'col'), may hold values from 0 to 15, as said below
- tile_count: int32 [256, 8], P('row', 'col'), may hold values from 1 to 2, as said below
Outputs:
- source_potential: float32 [65536], P('row')
- target_potential: float32 [32768], P('col')
Inputs may be any that keep to these rules, and one draw needn't show every extreme that they name: `tile_index`: within the 2 slots of one source tile and one index of col the target tiles are distinct; every target tile is named by a live slot of some source tile. `tile_count`: each index of row holds, for every index of col, a source tile with all 2 slots live.
All inputs are finite; a program needn't handle non-finite values.
Results may differ from a plain program's by a relative error of at most 0.0003.
Values may be sent and summed in bfloat16 or wider, within the bound.
A program may use at most 128 MiB of HBM per device.

v0:
```python
import math
import jax
import jax.numpy as jnp
from jax import lax
from jax.sharding import PartitionSpec as P

TILE = 256
ITERS = 3
masked_score = -1e30


def cost_terms(piece, source_points, tile_index):
    width = piece.shape[1]
    source_tiles = source_points.reshape(-1, TILE, width)
    target_tiles = piece.reshape(-1, TILE, width)
    chosen = target_tiles[tile_index]
    return jnp.einsum("rad,rkbd->rkab", source_tiles, chosen, preferred_element_type=jnp.float32)


def on_device(source_points, target_points, source_mass, target_mass, tile_index, tile_count):
    tiles_per_row = source_points.shape[0] // TILE
    col_tiles = target_points.shape[0] // TILE
    slot_count = tile_index.shape[1]
    scale = 1.0 / math.sqrt(source_points.shape[1])
    live = jnp.arange(slot_count)[None, :] < tile_count
    onehot = (tile_index[:, :, None] == jnp.arange(col_tiles)[None, None, :]) & live[:, :, None]
    log_source = jnp.log(source_mass).reshape(tiles_per_row, TILE)
    log_target = jnp.log(target_mass).reshape(col_tiles, TILE)
    target_pot = jnp.zeros((col_tiles, TILE), jnp.float32)
    source_pot = jnp.zeros((tiles_per_row, TILE), jnp.float32)
    for iteration in range(ITERS):
        cost = (
            cost_terms(
                lax.all_gather(target_points, "row", axis=1, tiled=True), source_points, tile_index
            )
            * scale
        )
        scores = cost + target_pot[tile_index][:, :, None, :]
        scores = jnp.where(live[:, :, None, None], scores, masked_score)
        row_top = jnp.max(scores, axis=(1, 3))
        highest = lax.pmax(row_top, "col")
        local_sum = jnp.sum(jnp.exp(scores - highest[:, None, :, None]), axis=(1, 3))
        total = lax.psum(local_sum, "col")
        source_pot = log_source - highest - jnp.log(total)
        columns = cost + source_pot[:, None, :, None]
        columns = jnp.where(live[:, :, None, None], columns, masked_score)
        slot_top = jnp.max(columns, axis=2)
        local_top = jnp.max(
            jnp.where(onehot[..., None], slot_top[:, :, None, :], masked_score), axis=(0, 1)
        )
        col_high = lax.pmax(local_top, "row")
        slot_ref = col_high[tile_index]
        sums = jnp.sum(jnp.exp(columns - slot_ref[:, :, None, :]), axis=2)
        col_sum = jnp.sum(jnp.where(onehot[..., None], sums[:, :, None, :], 0.0), axis=(0, 1))
        col_total = lax.psum(col_sum, "row")
        target_pot = log_target - col_high - jnp.log(col_total)
    return (source_pot.reshape(-1), target_pot.reshape(-1))


def solution(mesh):
    placed = (P("row", None), P("col", "row"), P("row"), P("col"), P("row", "col"), P("row", "col"))
    return jax.shard_map(
        on_device, mesh=mesh, in_specs=placed, out_specs=(P("row"), P("col")), check_vma=False
    )
```

profile of v0, /device:TPU:0, one launch (start us, length us, event | category | flops | bytes accessed | tf_op | source)
XLA Modules:
  0.0 747.5 jit_solution(9227641684370280702)
XLA Ops:
  7.2 0.7 all-gather.2.cloned.1.call-update
  7.9 0.8 copy.16
  8.7 0.7 compare_select_fusion
  9.5 0.6 gather_fusion.1
  10.2 0.7 log.24
  10.9 0.7 log.25
  11.6 0.7 iota_compare_fusion
  12.4 0.1 compare_and_fusion
  12.5 70.8 %all-gather.2.cloned.1.call-done = bf16[4096,1024]{0,1:T(8,128)(2,1)} async-done(((bf16[4096,64]{0,1:T(8,128)(2,1)}), bf16[4096,1024]{0,1:T(8,128)(2,1)}) %all-gather.2.cloned.1.call-update) | async-done | bytes 8388624 | tf_op jit(solution)/shard_map/all_gather | solution.py:34
  83.2 12.0 %copy.14 = bf16[4096,1024]{1,0:T(8,128)(2,1)} copy(bf16[4096,1024]{0,1:T(8,128)(2,1)} %all-gather.2.cloned.1.call-done) | data formatting | bytes 16777216 | tf_op jit(solution)/shard_map/all_gather | solution.py:34
  95.2 10.6 %gather_fusion = bf16[32,256,1024]{2,1,0:T(8,128)(2,1)} fusion(bf16[16,256,1024]{2,1,0:T(8,128)(2,1)} %bitcast.57, s32[1024]{0:T(1024)S(1)} %pad_clamp_fusion), kind=kCustom, calls=%fused_computation | custom fusion | bytes 33554560 | tf_op jit(solution)/shard_map/gather | solution.py:16
  105.8 13.5 %bitcast_reduce_fusion.5 = (f32[16,256]{1,0:T(8,128)S(1)}, f32[16,2,256,256]{3,2,1,0:T(8,128)}) fusion(f32[16,2,256]{2,1,0:T(2,128)S(1)} %reshape.108, pred[16,2]{1,0:T(8,128)(4,1)S(1)} %iota_compare_fusion, bf16[16,2,256,1024]{3,2,1,0:T(8,128)(2,1)} %bitcast.58, bf16[16,256,1024,1]{2,1,3,0:T(8,128)(2,1)} %bitcast.63), kind=kOutput, calls=%fused_computation.28 | convolution fusion | flops 4303351808 | bytes 33603616 | tf_op jit(solution)/shard_map/rad,rkbd->rkab/dot_general | solution.py:17
  119.3 25.8 %pmax.42 = f32[16,256]{1,0:T(8,128)S(1)} all-reduce(f32[16,256]{1,0:T(8,128)S(1)} %get-tuple-element.2), channel_id=1, replica_groups=mesh['row'=16,'col'=8] {'col'}, use_global_device_ids=true, to_apply=%region_1.2 | all-reduce | flops 4096 | bytes 32768 | tf_op jit(solution)/shard_map/pmax | solution.py:41
  145.1 4.6 fusion.11
  149.8 23.6 %psum.42 = f32[16,256]{1,0:T(8,128)S(1)} all-reduce(f32[16,256]{1,0:T(8,128)S(1)} %fusion.11), channel_id=1, replica_groups=mesh['row'=16,'col'=8] {'col'}, use_global_device_ids=true, to_apply=%region_3.4 | all-reduce | flops 4096 | bytes 32768 | tf_op jit(solution)/shard_map/psum | solution.py:43
  173.3 4.7 bitcast_reduce_fusion.4
  178.0 0.1 select_reduce_fusion.5
  178.1 72.4 %pmax.43 = f32[16,256]{1,0:T(8,128)S(1)} all-reduce(f32[16,256]{1,0:T(8,128)S(1)} %select_reduce_fusion.5), channel_id=1, replica_groups=mesh['row'=16,'col'=8] {'row'}, use_global_device_ids=true, to_apply=%region_6.7 | all-reduce | flops 4096 | bytes 32768 | tf_op jit(solution)/shard_map/pmax | solution.py:51
  250.5 0.6 gather_fusion.2
  251.1 5.1 fusion.9
  256.3 0.1 select_reduce_fusion.4
  256.4 69.5 %psum.43 = f32[16,256]{1,0:T(8,128)S(1)} all-reduce(f32[16,256]{1,0:T(8,128)S(1)} %select_reduce_fusion.4), channel_id=1, replica_groups=mesh['row'=16,'col'=8] {'row'}, use_global_device_ids=true, to_apply=%region_9.10 | all-reduce | flops 4096 | bytes 32768 | tf_op jit(solution)/shard_map/psum | solution.py:55
  326.0 0.6 gather_fusion.3
  326.6 4.4 bitcast_reduce_fusion.3
  331.0 23.7 %pmax.44 = f32[16,256]{1,0:T(8,128)S(1)} all-reduce(f32[16,256]{1,0:T(8,128)S(1)} %bitcast_reduce_fusion.3), channel_id=1, replica_groups=mesh['row'=16,'col'=8] {'col'}, use_global_device_ids=true, to_apply=%region_11.12 | all-reduce | flops 4096 | bytes 32768 | tf_op jit(solution)/shard_map/pmax | solution.py:41
  354.8 4.6 fusion.7
  359.4 23.6 %psum.44 = f32[16,256]{1,0:T(8,128)S(1)} all-reduce(f32[16,256]{1,0:T(8,128)S(1)} %fusion.7), channel_id=1, replica_groups=mesh['row'=16,'col'=8] {'col'}, use_global_device_ids=true, to_apply=%region_13.14 | all-reduce | flops 4096 | bytes 32768 | tf_op jit(solution)/shard_map/psum | solution.py:43
  383.0 4.7 bitcast_reduce_fusion.2
  387.6 0.1 select_reduce_fusion.3
  387.8 69.5 %pmax.45 = f32[16,256]{1,0:T(8,128)S(1)} all-reduce(f32[16,256]{1,0:T(8,128)S(1)} %select_reduce_fusion.3), channel_id=1, replica_groups=mesh['row'=16,'col'=8] {'row'}, use_global_device_ids=true, to_apply=%region_16.17 | all-reduce | flops 4096 | bytes 32768 | tf_op jit(solution)/shard_map/pmax | solution.py:51
  457.3 0.6 gather_fusion.4
  458.0 5.1 fusion.5
  463.1 0.1 select_reduce_fusion.2
  463.2 69.5 %psum.45 = f32[16,256]{1,0:T(8,128)S(1)} all-reduce(f32[16,256]{1,0:T(8,128)S(1)} %select_reduce_fusion.2), channel_id=1, replica_groups=mesh['row'=16,'col'=8] {'row'}, use_global_device_ids=true, to_apply=%region_19.20 | all-reduce | flops 4096 | bytes 32768 | tf_op jit(solution)/shard_map/psum | solution.py:55
  532.8 0.6 gather_fusion.5
  533.4 4.4 bitcast_reduce_fusion.1
  537.8 23.6 %pmax.46 = f32[16,256]{1,0:T(8,128)S(1)} all-reduce(f32[16,256]{1,0:T(8,128)S(1)} %bitcast_reduce_fusion.1), channel_id=1, replica_groups=mesh['row'=16,'col'=8] {'col'}, use_global_device_ids=true, to_apply=%region_21.22 | all-reduce | flops 4096 | bytes 32768 | tf_op jit(solution)/shard_map/pmax | solution.py:41
  561.4 4.6 fusion.3
  566.0 23.6 %psum.46 = f32[16,256]{1,0:T(8,128)S(1)} all-reduce(f32[16,256]{1,0:T(8,128)S(1)} %fusion.3), channel_id=1, replica_groups=mesh['row'=16,'col'=8] {'col'}, use_global_device_ids=true, to_apply=%region_23.24 | all-reduce | flops 4096 | bytes 32768 | tf_op jit(solution)/shard_map/psum | solution.py:43
  589.6 4.7 bitcast_reduce_fusion
  594.3 0.1 select_reduce_fusion.1
  594.4 69.5 %pmax.47 = f32[16,256]{1,0:T(8,128)S(1)} all-reduce(f32[16,256]{1,0:T(8,128)S(1)} %select_reduce_fusion.1), channel_id=1, replica_groups=mesh['row'=16,'col'=8] {'row'}, use_global_device_ids=true, to_apply=%region_26.27 | all-reduce | flops 4096 | bytes 32768 | tf_op jit(solution)/shard_map/pmax | solution.py:51
  663.9 0.6 gather_fusion.6
  664.6 5.1 fusion.1
  669.7 0.1 select_reduce_fusion
  669.8 69.5 %psum.47 = f32[16,256]{1,0:T(8,128)S(1)} all-reduce(f32[16,256]{1,0:T(8,128)S(1)} %select_reduce_fusion), channel_id=1, replica_groups=mesh['row'=16,'col'=8] {'row'}, use_global_device_ids=true, to_apply=%region_29.30 | all-reduce | flops 4096 | bytes 32768 | tf_op jit(solution)/shard_map/psum | solution.py:55
  739.4 0.6 copy.19
  740.0 0.6 copy.18
  (19 shorter events, 0.4 us)
Async XLA Ops:
  7.2 76.1 %all-gather.2.cloned.1.call-start = ((), (), s32[]{:S(2)}) async-start(), calls=%async_computation | async-start | bytes 8912896 | tf_op jit(solution)/shard_map/all_gather | solution.py:34
Sparse Core Ops, SparseCore 0:
  10.1 73.0 all-gather.1
where the time goes:
time: 748 us; the launch traced here: 747 us
  blocking collectives  564 us (75%)
  waiting for transfers between devices  71.4 us (10%)
  other arithmetic  54.5 us (7%)
  local copies, waits for them, and re-layouts  30 us (4%)
  between operations  14.3 us (2%)
  matrix products  13.5 us (2%)
    pmax x3, blocking collectives, on_device(): col_high = lax.pmax(local_top, 'row')  211 us
    psum x3, blocking collectives, on_device(): col_total = lax.psum(col_sum, 'row')  209 us
    pmax x3, blocking collectives, on_device(): highest = lax.pmax(row_top, 'col')  73.1 us
    all_gather x1, waiting for transfers between devices, on_device(): lax.all_gather(target_points, 'row', axis=1, tiled=True)  70.8 us
    psum x3, blocking collectives, on_device(): total = lax.psum(local_sum, 'col')  70.7 us
    reduce_sum x3, other arithmetic, on_device(): sums = jnp.sum(jnp.exp(columns - slot_ref[:, :, None, :]), axis=2)  15.4 us
  transfers between devices with their start and end apart: 1, of which 1 were waited for; matrix products, arithmetic and copies ran while one was open for 1% of the time, Pallas kernels for 0%

commit v1 on v0

--- a/solution.py
+++ b/solution.py
@@ -31,7 +31,12 @@
     for iteration in range(ITERS):
         cost = (
             cost_terms(
-                lax.all_gather(target_points, "row", axis=1, tiled=True), source_points, tile_index
+                jnp.concatenate(
+                    lax.all_to_all(jnp.stack([target_points] * lax.axis_size("row")), "row", 0, 0),
+                    axis=1,
+                ),
+                source_points,
+                tile_index,
             )
             * scale
         )

time: 748 us -> 827 us (1.11)
  waiting for transfers between devices: 71.4 us -> 146 us
  between operations: 14.3 us -> 0.95 us
  local copies, waits for them, and re-layouts: 30 us -> 43.2 us
    all_to_all x0 -> x1, waiting for transfers between devices: none -> 146 us  [on_device(): lax.all_to_all(jnp.stack([target_points] * lax.axis_size('row')), 'row',...]
    all_gather x1 -> x0, waiting for transfers between devices: 70.8 us -> none  [on_device(): lax.all_gather(target_points, 'row', axis=1, tiled=True)]
    another operation x0 -> x2, local copies, waits for them, and re-layouts: none -> 17.6 us  [the longest x1 12.2 us: cost_terms(): target_tiles = piece.reshape(-1, TILE, width)]
    all_gather x1 -> x0, local copies, waits for them, and re-layouts: 12 us -> none  [on_device(): lax.all_gather(target_points, 'row', axis=1, tiled=True)]
    unnamed x3 -> x12, local copies, waits for them, and re-layouts: 1.99 us -> 11 us
  transfers between devices with their start and end apart: 1 -> 1, of which waited for: 1 -> 1; matrix products, arithmetic and copies ran while one was open for 1% -> 0% of each run, Pallas kernels for 0% -> 0%
where the time goes in v1:
time: 827 us; the launch traced here: 826 us
  blocking collectives  561 us (68%)
  waiting for transfers between devices  146 us (18%)
  other arithmetic  53.2 us (6%)
  local copies, waits for them, and re-layouts  43.2 us (5%)
  matrix products  13.5 us (2%)
    pmax x3, blocking collectives, on_device(): col_high = lax.pmax(local_top, 'row')  210 us
    psum x3, blocking collectives, on_device(): col_total = lax.psum(col_sum, 'row')  209 us
    all_to_all x1, waiting for transfers between devices, on_device(): lax.all_to_all(jnp.stack([target_points] * lax.axis_size('row')), 'row',...  146 us
    pmax x3, blocking collectives, on_device(): highest = lax.pmax(row_top, 'col')  72.2 us
    psum x3, blocking collectives, on_device(): total = lax.psum(local_sum, 'col')  70.9 us
  transfers between devices with their start and end apart: 1, of which 1 were waited for; matrix products, arithmetic and copies ran while one was open for 0% of the time, Pallas kernels for 0%

profile of v1, /device:TPU:0, one launch (start us, length us, event | category | flops | bytes accessed | tf_op | source)
XLA Modules:
  0.0 826.0 jit_solution(9180183259429362478)
XLA Ops:
  0.6 5.3 stack.2
  6.0 7.3 all-to-all-start
  13.3 0.1 copy.19
  13.4 0.1 copy.17
  13.5 0.1 reshape.103
  13.6 0.6 gather_fusion.1
  14.4 0.1 compare_and_fusion
  14.5 146.5 %all-to-all-done = bf16[16,4096,64]{1,2,0:T(8,128)(2,1)} async-done(((bf16[16,4096,64]{1,2,0:T(8,128)(2,1)}), bf16[16,4096,64]{1,2,0:T(8,128)(2,1)}, u32[]{:S(2)}, u32[]{:S(2)}) %all-to-all-start) | async-done | bytes 8388640 | tf_op jit(solution)/shard_map/all_to_all | solution.py:35
  160.9 9.7 %copy.21 = bf16[128,8,16,256]{3,2,1,0:T(8,128)(2,1)} copy(bf16[128,8,16,256]{3,1,2,0:T(8,128)(2,1)} %bitcast.16) | data formatting | bytes 16777216
  170.6 12.2 %copy.18 = bf16[16,256,1024]{2,1,0:T(8,128)(2,1)} copy(bf16[16,256,1024]{1,0,2:T(8,128)(2,1)} %bitcast.62) | data formatting | bytes 16777216 | tf_op jit(solution)/shard_map/reshape;reshape | solution.py:15
  182.9 10.6 %gather_fusion = bf16[32,256,1024]{2,1,0:T(8,128)(2,1)} fusion(bf16[16,256,1024]{2,1,0:T(8,128)(2,1)} %copy.18, s32[1024]{0:T(1024)S(1)} %pad_clamp_fusion), kind=kCustom, calls=%fused_computation | custom fusion | bytes 33554560 | tf_op jit(solution)/shard_map/gather | solution.py:16
  193.5 13.5 %bitcast_reduce_fusion.5 = (f32[16,256]{1,0:T(8,128)S(1)}, f32[16,2,256,256]{3,2,1,0:T(8,128)}) fusion(f32[16,2,256]{2,1,0:T(2,128)S(1)} %reshape.110, pred[16,2]{1,0:T(8,128)(4,1)S(1)} %iota_compare_fusion, bf16[16,2,256,1024]{3,2,1,0:T(8,128)(2,1)} %bitcast.63, bf16[16,256,1024,1]{2,1,3,0:T(8,128)(2,1)} %bitcast.68), kind=kOutput, calls=%fused_computation.28 | convolution fusion | flops 4303351808 | bytes 33603616 | tf_op jit(solution)/shard_map/rad,rkbd->rkab/dot_general | solution.py:17
  207.0 25.1 %pmax.42 = f32[16,256]{1,0:T(8,128)S(1)} all-reduce(f32[16,256]{1,0:T(8,128)S(1)} %get-tuple-element.2), channel_id=1, replica_groups=mesh['row'=16,'col'=8] {'col'}, use_global_device_ids=true, to_apply=%region_1.2 | all-reduce | flops 4096 | bytes 32768 | tf_op jit(solution)/shard_map/pmax | solution.py:46
  232.1 4.6 fusion.11
  236.7 23.6 %psum.42 = f32[16,256]{1,0:T(8,128)S(1)} all-reduce(f32[16,256]{1,0:T(8,128)S(1)} %fusion.11), channel_id=1, replica_groups=mesh['row'=16,'col'=8] {'col'}, use_global_device_ids=true, to_apply=%region_3.4 | all-reduce | flops 4096 | bytes 32768 | tf_op jit(solution)/shard_map/psum | solution.py:48
  260.3 4.7 bitcast_reduce_fusion.4
  265.0 0.1 select_reduce_fusion.5
  265.1 70.8 %pmax.43 = f32[16,256]{1,0:T(8,128)S(1)} all-reduce(f32[16,256]{1,0:T(8,128)S(1)} %select_reduce_fusion.5), channel_id=1, replica_groups=mesh['row'=16,'col'=8] {'row'}, use_global_device_ids=true, to_apply=%region_6.7 | all-reduce | flops 4096 | bytes 32768 | tf_op jit(solution)/shard_map/pmax | solution.py:56
  335.9 0.6 gather_fusion.2
  336.5 5.1 fusion.9
  341.6 0.1 select_reduce_fusion.4
  341.8 69.5 %psum.43 = f32[16,256]{1,0:T(8,128)S(1)} all-reduce(f32[16,256]{1,0:T(8,128)S(1)} %select_reduce_fusion.4), channel_id=1, replica_groups=mesh['row'=16,'col'=8] {'row'}, use_global_device_ids=true, to_apply=%region_9.10 | all-reduce | flops 4096 | bytes 32768 | tf_op jit(solution)/shard_map/psum | solution.py:60
  411.3 0.6 gather_fusion.3
  411.9 4.4 bitcast_reduce_fusion.3
  416.4 23.6 %pmax.44 = f32[16,256]{1,0:T(8,128)S(1)} all-reduce(f32[16,256]{1,0:T(8,128)S(1)} %bitcast_reduce_fusion.3), channel_id=1, replica_groups=mesh['row'=16,'col'=8] {'col'}, use_global_device_ids=true, to_apply=%region_11.12 | all-reduce | flops 4096 | bytes 32768 | tf_op jit(solution)/shard_map/pmax | solution.py:46
  439.9 4.6 fusion.7
  444.6 23.6 %psum.44 = f32[16,256]{1,0:T(8,128)S(1)} all-reduce(f32[16,256]{1,0:T(8,128)S(1)} %fusion.7), channel_id=1, replica_groups=mesh['row'=16,'col'=8] {'col'}, use_global_device_ids=true, to_apply=%region_13.14 | all-reduce | flops 4096 | bytes 32768 | tf_op jit(solution)/shard_map/psum | solution.py:48
  468.1 4.7 bitcast_reduce_fusion.2
  472.8 0.1 select_reduce_fusion.3
  473.0 69.5 %pmax.45 = f32[16,256]{1,0:T(8,128)S(1)} all-reduce(f32[16,256]{1,0:T(8,128)S(1)} %select_reduce_fusion.3), channel_id=1, replica_groups=mesh['row'=16,'col'=8] {'row'}, use_global_device_ids=true, to_apply=%region_16.17 | all-reduce | flops 4096 | bytes 32768 | tf_op jit(solution)/shard_map/pmax | solution.py:56
  542.5 0.6 gather_fusion.4
  543.1 5.1 fusion.5
  548.3 0.1 select_reduce_fusion.2
  548.4 69.5 %psum.45 = f32[16,256]{1,0:T(8,128)S(1)} all-reduce(f32[16,256]{1,0:T(8,128)S(1)} %select_reduce_fusion.2), channel_id=1, replica_groups=mesh['row'=16,'col'=8] {'row'}, use_global_device_ids=true, to_apply=%region_19.20 | all-reduce | flops 4096 | bytes 32768 | tf_op jit(solution)/shard_map/psum | solution.py:60
  617.9 0.6 gather_fusion.5
  618.6 4.4 bitcast_reduce_fusion.1
  623.0 23.6 %pmax.46 = f32[16,256]{1,0:T(8,128)S(1)} all-reduce(f32[16,256]{1,0:T(8,128)S(1)} %bitcast_reduce_fusion.1), channel_id=1, replica_groups=mesh['row'=16,'col'=8] {'col'}, use_global_device_ids=true, to_apply=%region_21.22 | all-reduce | flops 4096 | bytes 32768 | tf_op jit(solution)/shard_map/pmax | solution.py:46
  646.6 4.6 fusion.3
  651.2 23.8 %psum.46 = f32[16,256]{1,0:T(8,128)S(1)} all-reduce(f32[16,256]{1,0:T(8,128)S(1)} %fusion.3), channel_id=1, replica_groups=mesh['row'=16,'col'=8] {'col'}, use_global_device_ids=true, to_apply=%region_23.24 | all-reduce | flops 4096 | bytes 32768 | tf_op jit(solution)/shard_map/psum | solution.py:48
  675.0 4.7 bitcast_reduce_fusion
  679.7 0.1 select_reduce_fusion.1
  679.8 69.5 %pmax.47 = f32[16,256]{1,0:T(8,128)S(1)} all-reduce(f32[16,256]{1,0:T(8,128)S(1)} %select_reduce_fusion.1), channel_id=1, replica_groups=mesh['row'=16,'col'=8] {'row'}, use_global_device_ids=true, to_apply=%region_26.27 | all-reduce | flops 4096 | bytes 32768 | tf_op jit(solution)/shard_map/pmax | solution.py:56
  749.3 0.6 gather_fusion.6
  750.0 5.1 fusion.1
  755.1 0.1 select_reduce_fusion
  755.2 69.5 %psum.47 = f32[16,256]{1,0:T(8,128)S(1)} all-reduce(f32[16,256]{1,0:T(8,128)S(1)} %select_reduce_fusion), channel_id=1, replica_groups=mesh['row'=16,'col'=8] {'row'}, use_global_device_ids=true, to_apply=%region_29.30 | all-reduce | flops 4096 | bytes 32768 | tf_op jit(solution)/shard_map/psum | solution.py:60
  824.8 0.6 copy.23
  825.4 0.6 copy.22
  (28 shorter events, 0.3 us)
Async XLA Ops:
  6.0 7.3 copy-start.2
  6.0 8.3 %copy-start = (f32[4096]{0:T(1024)S(1)}, f32[4096]{0:T(1024)}, u32[]{:S(2)}) copy-start(f32[4096]{0:T(1024)} %param.8) | copy-start | bytes 49156
  6.0 8.3 %copy-start.1 = (f32[4096]{0:T(1024)S(1)}, f32[4096]{0:T(1024)}, u32[]{:S(2)}) copy-start(f32[4096]{0:T(1024)} %param.9) | copy-start | bytes 49156
  6.0 8.3 %copy-start.3 = (s32[16,1]{0,1:T(1,128)S(1)}, s32[16,1]{0,1:T(1,128)}, u32[]{:S(2)}) copy-start(s32[16,1]{0,1:T(1,128)} %param.11) | copy-start | bytes 196
  6.0 155.0 %all-to-all-start = ((bf16[16,4096,64]{1,2,0:T(8,128)(2,1)}), bf16[16,4096,64]{1,2,0:T(8,128)(2,1)}, u32[]{:S(2)}, u32[]{:S(2)}) async-start(bf16[16,4096,64]{1,2,0:T(8,128)(2,1)} %stack.2), calls=%async_computation | async-start | bytes 16777216 | tf_op jit(solution)/shard_map/all_to_all | solution.py:35
